TPU v7x, 32 devices: a whole 2x2x4 slice. The times are simulated.
32 devices in a mesh: group: 2 (over y), head: 8 (over z, x), dp: 2 (over core).
Axes of the slice: x: 2, y: 2, z: 4, core: 2. Of those that a mesh axis runs over, the one named last changes fastest.
Arguments:
- queries: bfloat16 [32, 16384], P(('group', 'dp'), 'head'), parts along dimension 0, may hold values from -6 to 6
- new_kv: bfloat16 [32, 2, 1024], P(('group', 'dp')), parts along dimension 0, may hold values from -6 to 6
- positions: int32 [32], P(('group', 'dp')), parts along dimension 0, may hold values from 256 to 1023
- lengths: int32 [32], P(('group', 'dp')), parts along dimension 0, may hold values from 2 to 256, as said below
- kv_codes: bfloat16 [32, 2, 256, 1024], P(('group', 'dp'), None, 'head'), parts along dimension 0, may hold values from -8 to 7, as said below
- kv_scales: float32 [32, 2, 8, 256], P(('group', 'dp'), None, None, 'head'), parts along dimension 0, may hold values from 0.1 to 40
- wo_codes: bfloat16 [16384, 16384], P('head'), may hold values from -8 to 7, as said below
- wo_scales: float32 [16384], P('head'), may hold values from 0.004 to 0.03
- residual: bfloat16 [32, 16384], P(('group', 'dp'), 'head'), parts along dimension 0, may hold values from -6 to 6
Outputs:
- hidden_out: bfloat16 [32, 16384], P(('group', 'dp'), 'head'), parts along dimension 0
There are 2 independent parts, one for each index of `group`. A program takes and returns all parts, laid end to end along the dimension named above; an argument that names none is the same for every part. Nothing has to cross between parts.
Inputs may be any that keep to these rules, and one draw needn't show every extreme that they name: Each row has at least two live slots, which are slots 0 to lengths - 1 of every key-value head; some row is full (256 live slots). `kv_codes`: integer codes. `wo_codes`: integer codes.
All inputs are finite; a program needn't handle non-finite values.
Results may differ from a plain program's by a relative error of at most 0.0089.
Values may be sent and summed in bfloat16 or wider, within the bound.
A program may use at most 128 MiB of HBM per device.

v0:
```python
import functools

import jax
import jax.numpy as jnp
import numpy as np
from jax import lax
from jax.experimental import pallas as pl
from jax.experimental.pallas import tpu as pltpu
from jax.sharding import PartitionSpec as P

H = 128
KVH = 8
HD = 128


ROPE_BASE = 500000.0
NEG_FILL = -1e30


def partner_2(block, axis, distance):
    count = lax.axis_size(axis)
    route = []
    for low in range(count):
        high = low | 1 << distance
        if high != low and high < count:
            route += [(low, high), (high, low)]
    return lax.ppermute(block, axis, route)


def rotary(values_in, positions):
    half_dim = values_in.shape[-1] // 2
    inverse_rate = ROPE_BASE ** (
        -(jnp.arange(half_dim, dtype=jnp.float32) * (2.0 / values_in.shape[-1]))
    )
    angles = positions.astype(jnp.float32)[:, None, None] * inverse_rate
    cosine = jnp.cos(angles)
    sine_part = jnp.sin(angles)
    lower_half = values_in[..., :half_dim]
    upper_half = values_in[..., half_dim:]
    return jnp.concatenate(
        [
            lower_half * cosine - upper_half * sine_part,
            upper_half * cosine + lower_half * sine_part,
        ],
        axis=-1,
    )


def hadamard(size_needed):
    index_row = jnp.arange(size_needed, dtype=jnp.int32)
    common = jnp.bitwise_and(index_row[:, None], index_row[None, :])
    parity = jnp.zeros_like(common)
    for bit_pos in range(max(size_needed.bit_length() - 1, 0)):
        parity = parity + jnp.right_shift(common, bit_pos) % 2
    return jnp.where(parity % 2 == 0, 1.0, -1.0).astype(jnp.float32)


def settle(peak_source, total_source, summed_source, fresh_score, fresh_values):
    peak_final = jnp.maximum(jnp.max(peak_source, axis=1), fresh_score)
    rescale = jnp.exp(peak_source - peak_final[:, None])
    fresh_weight = jnp.exp(fresh_score - peak_final)
    total_final = jnp.sum(total_source * rescale, axis=1) + fresh_weight
    summed_final = (
        jnp.sum(summed_source * rescale[..., None], axis=1) + fresh_weight[..., None] * fresh_values
    )
    return (summed_final / total_final[..., None]).astype(jnp.bfloat16)


def on_device_general(
    queries, new_kv, positions, lengths, kv_codes, kv_scales, wo_codes, wo_scales, residual
):
    n_head = lax.axis_size("head")
    my_index = lax.axis_index("head")
    n_rows = queries.shape[0]
    heads_here = queries.shape[1] // HD
    group_size = H // KVH
    block_len = kv_codes.shape[2]
    first_slot = my_index * block_len
    score_scale = HD ** (-0.5)
    own_query = rotary(
        queries.reshape(n_rows, heads_here, HD).astype(jnp.float32), positions
    ).astype(jnp.bfloat16)
    all_query = lax.all_gather(
        own_query.reshape(n_rows, heads_here * HD), "head", axis=1, tiled=True
    )
    all_query = all_query.reshape(n_rows, KVH, group_size, HD)
    fresh_keys = rotary(
        new_kv[:, 0].reshape(n_rows, KVH, HD).astype(jnp.float32), positions
    ).astype(jnp.bfloat16)
    fresh_values = new_kv[:, 1].reshape(n_rows, KVH, HD).astype(jnp.float32)
    key_codes = kv_codes[:, 0].reshape(n_rows, block_len, KVH, HD)
    value_codes = kv_codes[:, 1].reshape(n_rows, block_len, KVH, HD).astype(jnp.float32)
    raw_scores = jnp.einsum(
        "rgjd,rtgd->rgjt", all_query, key_codes, preferred_element_type=jnp.float32
    )
    scores = raw_scores * kv_scales[:, 0][:, :, None, :] * score_scale
    slot_index = first_slot + jnp.arange(block_len, dtype=jnp.int32)
    is_valid = (slot_index[None, :] < lengths[:, None])[:, None, None, :]
    scores = jnp.where(is_valid, scores, NEG_FILL)
    peak_here = jnp.max(scores, axis=-1)
    weights = jnp.where(is_valid, jnp.exp(scores - peak_here[..., None]), 0.0)
    total_here = jnp.sum(weights, axis=-1)
    summed = jnp.einsum(
        "rgjt,rtgd->rgjd",
        weights * kv_scales[:, 1][:, :, None, :],
        value_codes,
        precision=lax.Precision.HIGHEST,
    )
    peak_full = peak_here.reshape(n_rows, H)
    total_full = total_here.reshape(n_rows, H)
    summed_full = summed.reshape(n_rows, H, HD)
    received = (
        lax.all_to_all(peak_full, "head", split_axis=1, concat_axis=1, tiled=True),
        lax.all_to_all(total_full, "head", split_axis=1, concat_axis=1, tiled=True),
        lax.all_to_all(summed_full, "head", split_axis=1, concat_axis=1, tiled=True),
    )
    peak_source = received[0].reshape(n_rows, n_head, heads_here)
    total_source = received[1].reshape(n_rows, n_head, heads_here)
    summed_source = received[2].reshape(n_rows, n_head, heads_here, HD)
    owned_group = my_index * heads_here // group_size
    key_owned = lax.dynamic_index_in_dim(fresh_keys, owned_group, 1, keepdims=False)
    fresh_score = (
        jnp.einsum("rjd,rd->rj", own_query, key_owned, preferred_element_type=jnp.float32)
        * score_scale
    )
    value_owned = lax.dynamic_index_in_dim(fresh_values, owned_group, 1, keepdims=False)
    fresh_spread = jnp.broadcast_to(value_owned[:, None, :], (n_rows, heads_here, HD))
    attended = settle(peak_source, total_source, summed_source, fresh_score, fresh_spread)
    local_table = hadamard(heads_here)
    rotated = jnp.einsum(
        "kj,rjd->rkd", local_table, attended.astype(jnp.float32), precision=lax.Precision.HIGHEST
    )
    for bit_pos in range(n_head.bit_length() - 1):
        partner = partner_2(rotated, "head", bit_pos)
        is_upper = jnp.right_shift(my_index, bit_pos) % 2 == 1
        rotated = jnp.where(is_upper, partner - rotated, rotated + partner)
    flat_rows = (rotated * H ** (-0.5)).reshape(n_rows, heads_here * HD).astype(jnp.bfloat16)
    partial_out = jnp.dot(flat_rows, wo_codes, preferred_element_type=jnp.float32)
    shares = lax.psum_scatter(partial_out, "head", scatter_dimension=1, tiled=True)
    return (residual.astype(jnp.float32) + shares * wo_scales).astype(jnp.bfloat16)


PEAK_FLOOR = -1e29
DEVICE = pl.DeviceIdType.MESH


def fused_kernel(
    n,
    positions_far,
    lengths_far,
    rates_far,
    queries_far,
    new_kv_far,
    kv_scales_far,
    kv_codes,
    wo_codes,
    out,
    positions,
    lengths,
    rates,
    queries,
    new_kv,
    kv_scales,
    in_sem,
    q_all,
    kv_here,
    scale_lanes,
    part_out,
    part_in,
    rot_out,
    rot_in,
    wo_here,
    share_out,
    share_in,
    kv_sem,
    wo_sem,
    q_send,
    q_recv,
    part_send,
    part_recv,
    rot_send,
    rot_recv,
    share_send,
    share_recv,
):
    me = lax.axis_index("head")
    core = lax.axis_index("dp")
    replica = lax.axis_index("group")
    n_rows = queries.shape[0]
    group = queries.shape[1] // HD
    block_len = kv_codes.shape[2]
    wide = wo_here.shape[2]
    half_wide = wide // 2
    halves = n_rows * block_len // HD
    rows_half = n_rows // halves
    score_scale = HD ** (-0.5)
    f32 = jnp.float32

    n_bits = n.bit_length() - 1
    bits = [lax.rem(lax.div(me, 2**b), 2) for b in range(n_bits)]
    peers = [
        sum((1 - bits[b] if step >> b & 1 else bits[b]) * 2**b for b in range(n_bits))
        for step in range(n)
    ]
    other_core = 1 - core

    def peer_of(step):
        return peers[step]

    def peer_at(step):
        peer = 0
        for b in range(n_bits):
            bit = lax.rem(lax.div(step, 2**b), 2)
            peer += (bits[b] + bit - 2 * bits[b] * bit) * 2**b
        return peer

    def side_of(other):
        return other_core if other else core

    def to(head, dp):
        return {"group": replica, "head": head, "dp": dp}

    fetched = [
        pltpu.make_async_copy(far, near, in_sem.at[k])
        for k, (far, near) in enumerate(
            [
                (positions_far, positions),
                (rates_far, rates),
                (queries_far, queries),
                (lengths_far, lengths),
                (kv_scales_far, kv_scales),
                (new_kv_far, new_kv),
            ]
        )
    ]
    for copy in fetched:
        copy.start()
    kv_copy = pltpu.make_async_copy(kv_codes, kv_here, kv_sem)
    kv_copy.start()

    def wo_copy(i):
        first = pl.multiple_of(i * (2 * wide) + core * wide, wide)
        return pltpu.make_async_copy(
            wo_codes.at[:, pl.ds(first, wide)], wo_here.at[i], wo_sem.at[i]
        )

    barrier = pltpu.get_barrier_semaphore()
    for step in range(n):
        for other in range(2):
            if step or other:
                pl.semaphore_signal(
                    barrier,
                    inc=1,
                    device_id=to(peer_of(step), side_of(other)),
                    device_id_type=DEVICE,
                )

    lane_1 = lax.broadcasted_iota(jnp.int32, (1, HD), 1)
    row_8 = lax.broadcasted_iota(jnp.int32, (n_rows, HD), 0)
    for copy in fetched[:3]:
        copy.wait()
    pos = jnp.zeros((n_rows, HD), f32)
    for r in range(n_rows):
        pos = jnp.where(row_8 == r, positions[r].astype(f32), pos)
    sign = jnp.where(lane_1 < HD // 2, -1.0, 1.0).astype(f32)
    angle = pos * rates[...]
    cosine = jnp.cos(angle)
    sine = jnp.sin(angle) * sign

    def turn(v, c, s):
        return v * c + pltpu.roll(v, HD // 2, 1) * s

    stacked = jnp.concatenate(
        [
            turn(queries[:, j * HD : (j + 1) * HD].astype(f32), cosine, sine)
            for j in range(group)
        ],
        axis=0,
    ).astype(jnp.bfloat16)

    def permutation(major, minor):
        size = major * minor
        to_row = lax.broadcasted_iota(jnp.int32, (size, size), 0)
        from_row = lax.broadcasted_iota(jnp.int32, (size, size), 1)
        shift = minor.bit_length() - 1
        wanted = (to_row & (minor - 1)) * major + (to_row >> shift)
        return jnp.where(wanted == from_row, 1.0, 0.0).astype(jnp.bfloat16)

    q_all[me] = jnp.dot(
        permutation(n_rows, group), stacked, preferred_element_type=f32
    ).astype(jnp.bfloat16)

    pl.semaphore_wait(barrier, 2 * n - 1)

    def q_copy(step):
        return pltpu.make_async_remote_copy(
            src_ref=q_all.at[me],
            dst_ref=q_all.at[me],
            send_sem=q_send.at[step],
            recv_sem=q_recv.at[me],
            device_id=to(peer_of(step), core),
            device_id_type=DEVICE,
        )

    def q_forward(step):
        block = peer_of(step)
        return pltpu.make_async_remote_copy(
            src_ref=q_all.at[block],
            dst_ref=q_all.at[block],
            send_sem=q_send.at[step + 1],
            recv_sem=q_recv.at[block],
            device_id=to(peer_of(1), core),
            device_id_type=DEVICE,
        )

    def q_arrival(source):
        return pltpu.make_async_remote_copy(
            src_ref=q_all.at[source],
            dst_ref=q_all.at[source],
            send_sem=q_send.at[0],
            recv_sem=q_recv.at[source],
            device_id=to(source, core),
            device_id_type=DEVICE,
        )

    direct = [1] + list(range(2, n, 2))
    for step in direct:
        q_copy(step).start()
    for step in (n - 1, n - 2):
        wo_copy(peer_of(step)).start()
    for copy in fetched[3:]:
        copy.wait()

    for which in range(2):
        for half in range(halves):
            scale_lanes[which, half] = jnp.concatenate(
                [
                    kv_scales[half * rows_half + r, which]
                    for r in range(rows_half)
                ],
                axis=1,
            ) * (score_scale if which == 0 else 1.0)
    shape = (rows_half * group, HD)
    row_of = lax.broadcasted_iota(jnp.int32, shape, 0) >> (group.bit_length() - 1)
    lane = lax.broadcasted_iota(jnp.int32, shape, 1)
    slot = me * block_len + (lane & (block_len - 1))
    lane_row = lane >> (block_len.bit_length() - 1)
    masks = []
    for half in range(halves):
        live = jnp.zeros(shape, jnp.int32)
        for r in range(rows_half):
            live = jnp.where(row_of == r, lengths[half * rows_half + r], live)
        masks.append(
            jnp.where(
                (row_of == lane_row) & (slot < live), 0.0, NEG_FILL
            ).astype(f32)
        )

    kv_copy.wait()

    def attend(g, stats):
        lanes = pl.ds(pl.multiple_of(g * HD, HD), HD)
        result = []
        for half in range(halves):
            first = half * rows_half
            keys = kv_here[first : first + rows_half, 0, :, lanes].reshape(HD, HD)
            values = kv_here[first : first + rows_half, 1, :, lanes].reshape(HD, HD)
            query = q_all[g, half * shape[0] : (half + 1) * shape[0], :]
            raw = lax.dot_general(
                query, keys, (((1,), (1,)), ((), ())), preferred_element_type=f32
            )
            scores = raw * scale_lanes[0, half, pl.ds(g, 1), :] + masks[half]
            peak = jnp.maximum(jnp.max(scores, axis=1, keepdims=True), PEAK_FLOOR)
            weights = jnp.exp(scores - peak)
            total = jnp.sum(weights, axis=1, keepdims=True)
            weighted = weights * scale_lanes[1, half, pl.ds(g, 1), :]
            summed = jnp.dot(
                weighted.astype(jnp.bfloat16), values, preferred_element_type=f32
            ).astype(jnp.bfloat16)
            part_out[first : first + rows_half, g + 1] = summed.reshape(
                rows_half, group, HD
            )
            stat = stats[half]
            stat = jnp.where(lane == g, peak, stat)
            result.append(jnp.where(lane == g + n, total, stat))
        return tuple(result)

    block = lax.div(me, n // 2)

    def part_copy(step, first, count):
        return pltpu.make_async_remote_copy(
            src_ref=part_out.at[peer_of(step), pl.ds(first, count)],
            dst_ref=part_in.at[me, pl.ds(first, count)],
            send_sem=part_send,
            recv_sem=part_recv,
            device_id=to(peer_of(step), core),
            device_id_type=DEVICE,
        )

    def arrivals(buffer, send, recv):
        return pltpu.make_async_remote_copy(
            src_ref=buffer.at[pl.ds(0, n - 1), pl.ds(0, n + 1)],
            dst_ref=buffer.at[pl.ds(0, n - 1), pl.ds(0, n + 1)],
            send_sem=send,
            recv_sem=recv,
            device_id=to(peer_of(1), core),
            device_id_type=DEVICE,
        )

    def send_part(last):
        if last:
            first, count = (1 - block) * (n // 2 + 1), n // 2 + 1
        else:
            first, count = block * (n // 2) + 1, n // 2
        for s in reversed(range(1, n)):
            part_copy(s, first, count).start()

    def await_q(step):
        q_arrival(peer_of(step)).wait_recv()

    stats = attend(me, tuple(jnp.zeros(shape, f32) for _ in range(halves)))
    for step in range(1, n, 2):
        if step + 1 < n:
            await_q(step + 1)
            q_forward(step + 1).start()
        await_q(step)
        stats = attend(peer_of(step), stats)
        if step + 1 < n:
            stats = attend(peer_of(step + 1), stats)
        else:
            for half in range(halves):
                for r in range(rows_half):
                    exact = stats[half][r * group : (r + 1) * group]
                    packed = jnp.zeros((group, HD), f32)
                    for piece in range(3):
                        rounded = exact.astype(jnp.bfloat16).astype(f32)
                        exact = exact - rounded
                        if piece:
                            rounded = pltpu.roll(rounded, piece * 2 * n, 1)
                        packed = packed + rounded
                    packed = packed.astype(jnp.bfloat16)
                    part_out[half * rows_half + r, 0] = packed
                    part_out[half * rows_half + r, n + 1] = packed
            send_part(True)
        if step == n // 2 - 1:
            send_part(False)
        if n - 2 - step >= 1:
            wo_copy(peer_of(n - 2 - step)).start()
        if n - 3 - step >= 0:
            wo_copy(peer_of(n - 3 - step)).start()
    part_in[me] = part_out[me]

    fresh_pair = new_kv[me].astype(f32)
    angle_me = positions[me].astype(f32) * rates[...]
    cosine_me = jnp.cos(angle_me)
    sine_me = jnp.sin(angle_me) * sign
    fresh_keys = [
        turn(
            jnp.broadcast_to(fresh_pair[0:1, g * HD : (g + 1) * HD], (8, HD)),
            cosine_me,
            sine_me,
        )[0:1].astype(jnp.bfloat16).astype(f32)
        for g in range(n)
    ]
    fresh_values = [fresh_pair[1:2, g * HD : (g + 1) * HD] for g in range(n)]

    common = lax.broadcasted_iota(jnp.int32, (H, H), 0) & lax.broadcasted_iota(
        jnp.int32, (H, H), 1
    )
    parity = jnp.zeros((H, H), jnp.int32)
    for b in range(H.bit_length() - 1):
        parity = parity ^ (lax.shift_right_logical(common, b) & 1)
    sylvester = jnp.where(parity == 0, 1.0, -1.0).astype(jnp.bfloat16)

    order = permutation(group, 2 * n_rows)
    lane_g = lax.broadcasted_iota(jnp.int32, (group, HD), 1)
    fresh = jnp.zeros((group, HD), f32)
    own_rows = pl.ds(pl.multiple_of(me * group, group), group)
    for g in range(n):
        score = jnp.sum(
            q_all[g, own_rows, :].astype(f32) * fresh_keys[g], axis=1, keepdims=True
        )
        fresh = jnp.where(lane_g == g, score * score_scale, fresh)

    arrivals(part_in, part_send, part_recv).wait_recv()
    stat = []
    for s in range(n):
        packed = part_in[s, n + 1 if s < n // 2 else 0].astype(f32)
        stat.append(
            packed
            + pltpu.roll(packed, HD - 2 * n, 1)
            + pltpu.roll(packed, HD - 4 * n, 1)
        )
    top = fresh
    for s in range(n):
        top = jnp.maximum(top, stat[s])
    factor = [jnp.exp(stat[s] - top) for s in range(n)]
    fresh_factor = jnp.exp(fresh - top)
    total = fresh_factor
    for s in range(n):
        total = total + factor[s] * pltpu.roll(stat[s], HD - n, 1)
    inverse = 1.0 / total
    factor = [f * inverse for f in factor]
    fresh_factor = fresh_factor * inverse

    attended = []
    for g in range(n):
        mixed = fresh_factor[:, g : g + 1] * fresh_values[g]
        for s in range(n):
            mixed = mixed + factor[s][:, g : g + 1] * part_in[s, g + 1].astype(f32)
        attended.append(mixed)
    attended = jnp.concatenate(attended, axis=0).astype(jnp.bfloat16)
    rotated = jnp.dot(sylvester, attended, preferred_element_type=f32) * (H ** (-0.5))
    rot_out[...] = rotated.astype(jnp.bfloat16).reshape(n, group, HD)

    def rot_copy(step, other):
        peer = peer_of(step)
        return pltpu.make_async_remote_copy(
            src_ref=rot_out.at[peer],
            dst_ref=rot_in.at[core, me],
            send_sem=rot_send.at[other],
            recv_sem=rot_recv.at[core],
            device_id=to(peer, side_of(other)),
            device_id_type=DEVICE,
        )

    def rot_arrival(other):
        side = side_of(other)
        count = pl.ds(0, n - 1 + other)
        return pltpu.make_async_remote_copy(
            src_ref=rot_out.at[count],
            dst_ref=rot_in.at[side, count],
            send_sem=rot_send.at[other],
            recv_sem=rot_recv.at[side],
            device_id=to(peer_of(1), side),
            device_id_type=DEVICE,
        )

    pairs = [(s, o) for s in reversed(range(n)) for o in range(2) if s or o]
    for step, other in pairs:
        rot_copy(step, other).start()
    rot_in[core, me] = rot_out[me]
    for other in range(2):
        rot_arrival(other).wait_recv()
    tiles = jnp.dot(
        order, rot_in[...].reshape(2 * n_rows * group, HD), preferred_element_type=f32
    ).astype(jnp.bfloat16)
    flat_rows = jnp.concatenate(
        [tiles[k * 2 * n_rows : (k + 1) * 2 * n_rows] for k in range(group)], axis=1
    )

    def share_copy(i, other):
        side = side_of(other)
        return pltpu.make_async_remote_copy(
            src_ref=share_out.at[side, i],
            dst_ref=share_in.at[core, me],
            send_sem=share_send.at[other],
            recv_sem=share_recv.at[core],
            device_id=to(i, side),
            device_id_type=DEVICE,
        )

    def share_arrival(other):
        side = side_of(other)
        count = pl.ds(0, n - 1 + other)
        return pltpu.make_async_remote_copy(
            src_ref=share_out.at[side, count],
            dst_ref=share_in.at[side, count],
            send_sem=share_send.at[other],
            recv_sem=share_recv.at[side],
            device_id=to(peer_of(1), side),
            device_id_type=DEVICE,
        )

    def project(i):
        wo_copy(i).wait()
        share = jnp.dot(flat_rows, wo_here[i], preferred_element_type=f32)
        for side in range(2):
            rows = share[side * n_rows : (side + 1) * n_rows]
            share_out[side, i] = jnp.concatenate(
                [rows[:, :half_wide], rows[:, half_wide:]], axis=0
            ).astype(jnp.bfloat16)

    def project_step(step, carry):
        i = peer_at(n - step)
        project(i)
        share_copy(i, 0).start()
        share_copy(i, 1).start()
        return carry

    lax.fori_loop(1, n, project_step, 0)
    project(me)
    share_copy(me, 1).start()
    share_in[core, me] = share_out[core, me]

    for other in range(2):
        share_arrival(other).wait_recv()
    for side in range(2):
        added = share_in[side, 0].astype(f32)
        for s in range(1, n):
            added = added + share_in[side, s].astype(f32)
        for half in range(2):
            first = side * wide + half * half_wide
            out[:, first : first + half_wide] = added[half * n_rows : (half + 1) * n_rows]

    for step in direct:
        q_copy(step).wait_send()
    for step in direct[1:]:
        q_forward(step).wait_send()
    arrivals(part_out, part_send, part_recv).wait_send()
    for other in range(2):
        rot_arrival(other).wait_send()
        share_arrival(other).wait_send()


def on_device_fused(
    queries, new_kv, positions, lengths, kv_codes, kv_scales, wo_codes, wo_scales, residual
):
    n = lax.axis_size("head")
    n_rows = queries.shape[0]
    group = queries.shape[1] // HD
    block_len = kv_codes.shape[2]
    width = wo_codes.shape[1]
    wide = width // n // 2
    halves = n_rows * block_len // HD
    rates = ROPE_BASE ** (-np.arange(HD // 2) * (2.0 / HD))
    rates = np.tile(rates, 2)[None, :].astype(np.float32)
    bf16, f32 = jnp.bfloat16, jnp.float32
    vmem = pl.BlockSpec(memory_space=pltpu.VMEM)
    hbm = pl.BlockSpec(memory_space=pltpu.HBM)
    dma = pltpu.SemaphoreType.DMA
    shares = pl.pallas_call(
        functools.partial(fused_kernel, n),
        out_shape=jax.ShapeDtypeStruct(residual.shape, f32),
        in_specs=[hbm] * 8,
        out_specs=vmem,
        scratch_shapes=[
            pltpu.SMEM(positions.shape, jnp.int32),
            pltpu.SMEM(lengths.shape, jnp.int32),
            pltpu.VMEM(rates.shape, f32),
            pltpu.VMEM(queries.shape, bf16),
            pltpu.VMEM(new_kv.shape, bf16),
            pltpu.VMEM(kv_scales.shape, f32),
            dma((6,)),
            pltpu.VMEM((n, n_rows * group, HD), bf16),
            pltpu.VMEM(kv_codes.shape, bf16),
            pltpu.VMEM((2, halves, KVH, HD), f32),
            pltpu.VMEM((n, n + 2, group, HD), bf16),
            pltpu.VMEM((n, n + 2, group, HD), bf16),
            pltpu.VMEM((n, group, HD), bf16),
            pltpu.VMEM((2, n, group, HD), bf16),
            pltpu.VMEM((n, wo_codes.shape[0], wide), bf16),
            pltpu.VMEM((2, n, 2 * n_rows, wide // 2), bf16),
            pltpu.VMEM((2, n, 2 * n_rows, wide // 2), bf16),
            dma,
            dma((n,)),
            dma((n + 1,)),
            dma((n,)),
            dma,
            dma,
            dma((2,)),
            dma((2,)),
            dma((2,)),
            dma((2,)),
        ],
        compiler_params=pltpu.CompilerParams(
            collective_id=0, has_side_effects=True, vmem_limit_bytes=64 * 1024 * 1024
        ),
        cost_estimate=pl.CostEstimate(
            flops=2 * 2 * n_rows * wo_codes.shape[0] * width // 2,
            bytes_accessed=wo_codes.shape[0] * width,
            transcendentals=0,
        ),
    )(
        positions,
        lengths,
        rates,
        queries,
        new_kv,
        kv_scales,
        kv_codes,
        wo_codes,
    )
    return (residual.astype(f32) + shares * wo_scales).astype(bf16)


def on_device(*arrays):
    queries, kv_codes, wo_codes = arrays[0], arrays[4], arrays[6]
    n = lax.axis_size("head")
    n_rows, group, block_len = queries.shape[0], queries.shape[1] // HD, kv_codes.shape[2]
    fits = (
        lax.axis_size("dp") == 2
        and n == KVH == n_rows
        and n & (n - 1) == 0
        and group == H // KVH == 16
        and block_len % 16 == 0
        and block_len < HD
        and HD % block_len == 0
        and n_rows * block_len % HD == 0
        and wo_codes.shape[1] % (n * 512) == 0
    )
    return (on_device_fused if fits else on_device_general)(*arrays)


def solution(mesh):
    placed = (
        P(("group", "dp"), "head"),
        P(("group", "dp"), None, None),
        P(("group", "dp")),
        P(("group", "dp")),
        P(("group", "dp"), None, "head", None),
        P(("group", "dp"), None, None, "head"),
        P("head", None),
        P("head"),
        P(("group", "dp"), "head"),
    )
    return jax.shard_map(
        on_device, mesh=mesh, in_specs=placed, out_specs=P(("group", "dp"), "head"), check_vma=False
    )
```

profile of v0, /device:TPU:0, one launch (start us, length us, event | category | flops | bytes accessed | tf_op | source)
XLA Modules:
  0.0 37.8 jit_solution(850010515025634426)
XLA Ops:
  0.0 36.3 %shard_map.100 = f32[8,2048]{1,0:T(8,128)} custom-call(s32[8]{0:T(128)} %positions_far.1, s32[8]{0:T(128)} %lengths_far.1, f32[1,128]{1,0:T(1,128)} %constant.2.clone.rates_far, bf16[8,2048]{1,0:T(8,128)(2,1)} %queries_far.1, bf16[8,2,1024]{2,1,0:T(2,128)(2,1)} %new_kv_far.1, f32[8,2,8,32]{3,2,1,0:T(8,128)} %kv_scales_far.1, ...), custom_call_target="tpu_custom_call" | custom-call | flops 536870912 | bytes 33554432 | tf_op jit(solution)/shard_map/pallas_call | solution.py:632
  36.3 1.5 %add_convert_fusion = bf16[8,2048]{1,0:T(8,128)(2,1)} fusion(f32[8,2048]{1,0:T(8,128)} %shard_map.100, bf16[8,2048]{1,0:T(8,128)(2,1)} %param.18, f32[2048]{0:T(1024)} %param.17), kind=kLoop, calls=%fused_computation | loop fusion | flops 65536 | bytes 139264 | tf_op jit(solution)/shard_map/convert_element_type | solution.py:684
where the time goes:
time: 38 us; the launch traced here: 37.8 us
  Pallas kernels  36.3 us (96%)
  other arithmetic  1.49 us (4%)
    pallas_call x1, Pallas kernels, on_device_fused(): pl.pallas_call(functools.partial(fused_kernel, n), out_shape=jax.ShapeDty...  36.3 us
    convert_element_type x1, other arithmetic, on_device_fused(): return (residual.astype(f32) + shares * wo_scales).astype(bf16)  1.49 us

commit v1 on v0

--- a/solution.py
+++ b/solution.py
@@ -572,24 +572,31 @@
             device_id_type=DEVICE,
         )
 
-    def project(i):
-        wo_copy(i).wait()
-        share = jnp.dot(flat_rows, wo_here[i], preferred_element_type=f32)
-        for side in range(2):
-            rows = share[side * n_rows : (side + 1) * n_rows]
-            share_out[side, i] = jnp.concatenate(
-                [rows[:, :half_wide], rows[:, half_wide:]], axis=0
-            ).astype(jnp.bfloat16)
+    def project(pair):
+        for i in pair:
+            wo_copy(i).wait()
+        shares = [
+            jnp.dot(flat_rows, wo_here[i], preferred_element_type=f32) for i in pair
+        ]
+        for i, share in zip(pair, shares):
+            for side in range(2):
+                rows = share[side * n_rows : (side + 1) * n_rows]
+                share_out[side, i] = jnp.concatenate(
+                    [rows[:, :half_wide], rows[:, half_wide:]], axis=0
+                ).astype(jnp.bfloat16)
 
     def project_step(step, carry):
-        i = peer_at(n - step)
-        project(i)
-        share_copy(i, 0).start()
-        share_copy(i, 1).start()
+        pair = [peer_at(n - 1 - 2 * step), peer_at(n - 2 - 2 * step)]
+        project(pair)
+        for i in pair:
+            share_copy(i, 0).start()
+            share_copy(i, 1).start()
         return carry
 
-    lax.fori_loop(1, n, project_step, 0)
-    project(me)
+    lax.fori_loop(0, n // 2 - 1, project_step, 0)
+    project([peers[1], me])
+    share_copy(peers[1], 0).start()
+    share_copy(peers[1], 1).start()
     share_copy(me, 1).start()
     share_in[core, me] = share_out[core, me]
 

time: 38 us -> 38.3 us (level)
  Pallas kernels: 36.3 us -> 36.7 us
where the time goes in v1:
time: 38.3 us; the launch traced here: 38.2 us
  Pallas kernels  36.7 us (96%)
  other arithmetic  1.49 us (4%)
    pallas_call x1, Pallas kernels, on_device_fused(): pl.pallas_call(functools.partial(fused_kernel, n), out_shape=jax.ShapeDty...  36.7 us
    convert_element_type x1, other arithmetic, on_device_fused(): return (residual.astype(f32) + shares * wo_scales).astype(bf16)  1.49 us

profile of v1, /device:TPU:0, one launch (start us, length us, event | category | flops | bytes accessed | tf_op | source)
XLA Modules:
  0.0 38.2 jit_solution(13469281536032627751)
XLA Ops:
  0.0 36.7 %shard_map.100 = f32[8,2048]{1,0:T(8,128)} custom-call(s32[8]{0:T(128)} %positions_far.1, s32[8]{0:T(128)} %lengths_far.1, f32[1,128]{1,0:T(1,128)} %constant.2.clone.rates_far, bf16[8,2048]{1,0:T(8,128)(2,1)} %queries_far.1, bf16[8,2,1024]{2,1,0:T(2,128)(2,1)} %new_kv_far.1, f32[8,2,8,32]{3,2,1,0:T(8,128)} %kv_scales_far.1, ...), custom_call_target="tpu_custom_call" | custom-call | flops 536870912 | bytes 33554432 | tf_op jit(solution)/shard_map/pallas_call | solution.py:639
  36.7 1.5 %add_convert_fusion = bf16[8,2048]{1,0:T(8,128)(2,1)} fusion(f32[8,2048]{1,0:T(8,128)} %shard_map.100, bf16[8,2048]{1,0:T(8,128)(2,1)} %param.18, f32[2048]{0:T(1024)} %param.17), kind=kLoop, calls=%fused_computation | loop fusion | flops 65536 | bytes 139264 | tf_op jit(solution)/shard_map/convert_element_type | solution.py:691
